TPU v7x, 512 devices: a whole 4x4x16 slice. The times are simulated.
512 devices in a mesh: dp: 64 (over x, z), mp: 8 (over y, core).
Axes of the slice: x: 4, y: 4, z: 16, core: 2. Of those that a mesh axis runs over, the one named last changes fastest.
Arguments:
- queries: bfloat16 [65536, 2048], P(('dp', 'mp')), may hold values from -8 to 8
- encoder_keys: bfloat16 [73728, 2048], P('dp', 'mp'), may hold values from -8 to 8
- encoder_values: bfloat16 [73728, 2048], P('dp', 'mp'), may hold values from -6 to 6
- context_grad: bfloat16 [65536, 2048], P(('dp', 'mp')), may hold values from -6 to 6
- encoder_lengths: int32 [64, 2], replicated, may hold values from 288 to 576, as said below
- decoder_lengths: int32 [64, 2], replicated, may hold values from 128 to 512, as said below
- target_device: int32 [64, 2], replicated, may hold values from 0 to 63, as said below
Outputs:
- context: bfloat16 [65536, 2048], P(('dp', 'mp'))
- query_grad: bfloat16 [65536, 2048], P(('dp', 'mp'))
- key_grad: bfloat16 [73728, 2048], P('dp', 'mp')
- value_grad: bfloat16 [73728, 2048], P('dp', 'mp')
Inputs may be any that keep to these rules, and one draw needn't show every extreme that they name: target_device[a, k] = (a + s_k) mod 64 with one shift s_k for each column; the shifts are 1 or more and add up to 63. `encoder_lengths`: each row has an entry equal to 576. `decoder_lengths`: each row has an entry equal to 512.
All inputs are finite; a program needn't handle non-finite values.
Results may differ from a plain program's by a relative error of at most 0.011.
Values may be sent and summed in bfloat16 or wider, within the bound.
No kernel may reach another device: no remote copies, remote signals or barrier semaphores. Data moves between devices by JAX's collectives and lax.ppermute only.
A program may use at most 64 MiB of HBM per device.

v0:
```python
import functools

import jax
import jax.numpy as jnp
from jax import lax
from jax.experimental import pallas as pl
from jax.experimental.pallas import tpu as pltpu
from jax.sharding import PartitionSpec as P

HEAD_DIM = 256
SCALING = HEAD_DIM ** (-0.5)
ROWS = 256
RING = 16
KEY_HOPS = 2
SMEM = pl.BlockSpec(memory_space=pltpu.SMEM)
NT = (((1,), (1,)), ((), ()))
TN = (((0,), (0,)), ((), ()))
WAY, AROUND, COL, DEC_LEN, ENC_LEN, KEY_LEN, QUERY_LEN = 0, 1, 2, 4, 6, 8, 10
PARAMS = pltpu.CompilerParams(vmem_limit_bytes=32 * 2**20)


def dot(a, b, dims=(((1,), (0,)), ((), ()))):
    return lax.dot_general(a, b, dims, preferred_element_type=jnp.float32)


def passed_along(block, distance):
    owners = lax.axis_size("dp")
    if distance % owners == 0:
        return block
    return lax.ppermute(block, "dp", [(i, (i + distance) % owners) for i in range(owners)])


def one_hot(shape, gap, live):
    row = lax.broadcasted_iota(jnp.int32, shape, 0)
    col = lax.broadcasted_iota(jnp.int32, shape, 1)
    return ((col - row == gap) & (col < live)).astype(jnp.float32).astype(jnp.bfloat16)


def unpacked(m, len0, len1, arrays, m_ref, n_ref):
    total, cap = arrays[0].shape[0], m_ref.shape[1]
    pick = one_hot((cap, total), len0, len0 + len1)
    live = lax.broadcasted_iota(jnp.int32, (cap, 1), 0) < len0
    for c, rows in enumerate(arrays):
        first = jnp.where(live, rows[:cap], jnp.zeros_like(rows[:cap]))
        second = dot(pick, rows).astype(rows.dtype)
        m_ref[c] = jnp.where(m == 0, first, second)
        n_ref[c] = jnp.where(m == 0, second, first)


def packed(m, len0, len1, a, b, total):
    cap = a.shape[0]
    first = jnp.where(m == 0, a, b)
    second = jnp.where(m == 0, b, a)
    live = lax.broadcasted_iota(jnp.int32, (cap, 1), 0) < len0
    first = jnp.where(live, first, jnp.zeros_like(first)).astype(jnp.float32)
    moved = dot(one_hot((total, cap), -len0, len1), second)
    return jnp.concatenate([moved[:cap] + first, moved[cap:]], axis=0).astype(a.dtype)


def prepare_kernel(owners, own_ref, enc_ref, dec_ref, target_ref, k_ref, v_ref, out_ref, kvm_ref, kvn_ref):
    own = own_ref[0]
    shift0 = lax.rem(target_ref[0, 0], owners)
    m = jnp.where(lax.rem(shift0, RING) < RING // 2, 0, 1)
    shift = jnp.where(m == 0, shift0, owners - 1 - shift0)
    h = lax.rem(shift, RING)
    k = lax.div(shift, RING)
    out_ref[WAY] = k * (KEY_HOPS + 1) + jnp.minimum(h, KEY_HOPS) - 1
    out_ref[AROUND] = jnp.maximum(h, KEY_HOPS - 1) - (KEY_HOPS - 1)
    out_ref[COL] = m
    out_ref[COL + 1] = 0

    def wrapped(i):
        return lax.rem(i + 2 * owners, owners)

    for n in range(2):
        col = m if n == 0 else 1 - m
        sign = 1 - 2 * n
        hops = jnp.minimum(h + n, KEY_HOPS)
        out_ref[DEC_LEN + n] = dec_ref[n, own]
        out_ref[ENC_LEN + n] = enc_ref[n, own]
        out_ref[KEY_LEN + n] = enc_ref[col, wrapped(own - sign * (RING * k + hops))]
        out_ref[QUERY_LEN + n] = dec_ref[col, wrapped(own + sign * (h + n - hops))]
    for n in range(QUERY_LEN + 2, out_ref.shape[0]):
        out_ref[n] = 0
    unpacked(m, enc_ref[0, own], enc_ref[1, own], (k_ref[...], v_ref[...]), kvm_ref, kvn_ref)


def prepare(own, enc, dec, target, keys, values, owners, cap):
    slot = jax.ShapeDtypeStruct((2, cap, HEAD_DIM), keys.dtype)
    return pl.pallas_call(
        functools.partial(prepare_kernel, owners),
        in_specs=[SMEM] * 4 + [pl.BlockSpec()] * 2,
        out_specs=[SMEM] + [pl.BlockSpec()] * 2,
        out_shape=[jax.ShapeDtypeStruct((16,), jnp.int32), slot, slot],
        compiler_params=PARAMS,
    )(own, enc, dec, target, keys, values)


def split_kernel(q_ref, g_ref, parts_ref):
    for j in range(parts_ref.shape[0]):
        for c, in_ref in enumerate((q_ref, g_ref)):
            parts_ref[j, c] = in_ref[:, j * HEAD_DIM : (j + 1) * HEAD_DIM]


def split(queries, grads):
    rows, width = queries.shape
    return pl.pallas_call(
        split_kernel,
        out_shape=jax.ShapeDtypeStruct((width // HEAD_DIM, 2, rows, HEAD_DIM), queries.dtype),
        compiler_params=PARAMS,
    )(queries, grads)


def join_kernel(parts_ref, *outs):
    for j in range(parts_ref.shape[0]):
        for c, out_ref in enumerate(outs):
            out_ref[:, j * HEAD_DIM : (j + 1) * HEAD_DIM] = parts_ref[j, c]


def join(parts):
    heads, count, rows, _ = parts.shape
    return pl.pallas_call(
        join_kernel,
        out_shape=[jax.ShapeDtypeStruct((rows, heads * HEAD_DIM), parts.dtype)] * count,
        compiler_params=PARAMS,
    )(parts)


def pack_kernel(scal, in_ref, xm_ref, xn_ref):
    size, count, rows, _ = in_ref.shape
    m, len0, len1 = scal[COL], scal[DEC_LEN], scal[DEC_LEN + 1]

    def part(j, _):
        base = pl.multiple_of(j * rows, rows)
        at = pl.ds(base, rows)
        pick = one_hot((rows, size * rows), len0 + base, len0 + len1)
        live = lax.broadcasted_iota(jnp.int32, (rows, 1), 0) + base < len0
        for c in range(count):
            first = in_ref[j, c]
            first = jnp.where(live, first, jnp.zeros_like(first))
            second = dot(pick, in_ref[:, c].reshape(size * rows, HEAD_DIM)).astype(first.dtype)
            xm_ref[c, at, :] = jnp.where(m == 0, first, second)
            xn_ref[c, at, :] = jnp.where(m == 0, second, first)
        return 0

    lax.fori_loop(0, xm_ref.shape[1] // rows, part, 0)


def pack(scal, parts, cap):
    slot = jax.ShapeDtypeStruct((parts.shape[1], cap, HEAD_DIM), parts.dtype)
    return pl.pallas_call(
        pack_kernel,
        in_specs=[SMEM, pl.BlockSpec()],
        out_shape=[slot, slot],
        compiler_params=PARAMS,
    )(scal, parts)


def merge_parts_kernel(scal, a_ref, b_ref, parts_ref):
    size, count, rows, _ = parts_ref.shape
    cap = a_ref.shape[1]
    m, len0, len1 = scal[COL], scal[DEC_LEN], scal[DEC_LEN + 1]

    def part(j, _):
        base = j * rows
        at = pl.ds(pl.multiple_of(jnp.minimum(base, cap - rows), rows), rows)
        live = lax.broadcasted_iota(jnp.int32, (rows, 1), 0) + base < len0
        pick = one_hot((rows, cap), -len0 + base, len1)
        for c in range(count):
            first = jnp.where(m == 0, a_ref[c, at, :], b_ref[c, at, :])
            second = jnp.where(m == 0, b_ref[c], a_ref[c])
            first = jnp.where(live, first, jnp.zeros_like(first)).astype(jnp.float32)
            parts_ref[j, c] = (dot(pick, second) + first).astype(parts_ref.dtype)
        return 0

    lax.fori_loop(0, size, part, 0)


def merge_parts(scal, a, b, parts):
    rows = a.shape[1] * 2 // parts
    return pl.pallas_call(
        merge_parts_kernel,
        in_specs=[SMEM, pl.BlockSpec(), pl.BlockSpec()],
        out_shape=jax.ShapeDtypeStruct((parts, a.shape[0], rows, HEAD_DIM), a.dtype),
        compiler_params=PARAMS,
    )(scal, a, b)


def merge_keys_kernel(scal, a_ref, b_ref, *outs):
    for c, out_ref in enumerate(outs):
        rows = packed(scal[COL], scal[ENC_LEN], scal[ENC_LEN + 1], a_ref[c], b_ref[c], out_ref.shape[0])
        out_ref[...] = rows


def merge_keys(scal, a, b, total):
    return pl.pallas_call(
        merge_keys_kernel,
        in_specs=[SMEM, pl.BlockSpec(), pl.BlockSpec()],
        out_shape=[jax.ShapeDtypeStruct((total, HEAD_DIM), a.dtype)] * a.shape[0],
        compiler_params=PARAMS,
    )(scal, a, b)


def attend_kernel(n, scal, x_ref, kv_ref, y_ref, dkv_ref, acc_ref):
    step = pl.program_id(0)
    rows = x_ref.shape[1]
    valid = lax.broadcasted_iota(jnp.int32, (rows, 1), 0) + step * rows < scal[QUERY_LEN + n]
    q, g, keys, values = x_ref[0], x_ref[1], kv_ref[0], kv_ref[1]
    scores = dot(q, keys, NT) * SCALING
    col = lax.broadcasted_iota(jnp.int32, (1, scores.shape[1]), 1)
    scores = jnp.where(col < scal[KEY_LEN + n], scores, -1e30)
    raised = jnp.exp(scores - jnp.max(scores, axis=1, keepdims=True))
    probs = raised * (1.0 / jnp.sum(raised, axis=1, keepdims=True))
    probs_b = probs.astype(jnp.bfloat16)
    prob_grad = dot(g, values, NT)
    row_dot = jnp.sum(probs * prob_grad, axis=1, keepdims=True)
    score_grad = (probs * (prob_grad - row_dot)).astype(jnp.bfloat16)
    y_ref[0] = jnp.where(valid, dot(probs_b, values), 0.0).astype(y_ref.dtype)
    y_ref[1] = jnp.where(valid, dot(score_grad, keys) * SCALING, 0.0).astype(y_ref.dtype)

    @pl.when(step == 0)
    def _():
        acc_ref[...] = jnp.zeros_like(acc_ref)

    acc_ref[0] += dot(score_grad, q, TN)
    acc_ref[1] += dot(probs_b, g, TN)

    @pl.when(step == pl.num_programs(0) - 1)
    def _():
        dkv_ref[0] = (acc_ref[0] * SCALING).astype(dkv_ref.dtype)
        dkv_ref[1] = acc_ref[1].astype(dkv_ref.dtype)


def attend(n, scal, x, kv):
    cap, keys = x.shape[1], kv.shape[1]
    blocks = pl.BlockSpec((2, ROWS, HEAD_DIM), lambda i: (0, i, 0))
    whole = pl.BlockSpec(kv.shape, lambda i: (0, 0, 0))
    return pl.pallas_call(
        functools.partial(attend_kernel, n),
        grid=(cap // ROWS,),
        in_specs=[SMEM, blocks, whole],
        out_specs=[blocks, whole],
        out_shape=[jax.ShapeDtypeStruct(x.shape, x.dtype), jax.ShapeDtypeStruct(kv.shape, kv.dtype)],
        scratch_shapes=[pltpu.VMEM(kv.shape, jnp.float32)],
        compiler_params=PARAMS,
        cost_estimate=pl.CostEstimate(
            flops=12 * cap * keys * HEAD_DIM, bytes_accessed=3 * 2**20, transcendentals=cap * keys
        ),
    )(scal, x, kv)


def exchanged(parts, flag):
    def swap(parts):
        return lax.all_to_all(parts, "mp", split_axis=0, concat_axis=0, tiled=True)

    return lax.cond(flag, swap, lambda parts: parts, parts)


def local(
    queries,
    encoder_keys,
    encoder_values,
    context_grad,
    encoder_lengths,
    decoder_lengths,
    target_device,
):
    owners = lax.axis_size("dp")
    own = lax.axis_index("dp").astype(jnp.int32).reshape(1)
    seq_count = target_device.shape[1]
    dec_total = queries.shape[0] * lax.axis_size("mp")
    dec_cap = dec_total // seq_count
    enc_total = encoder_keys.shape[0]
    enc_cap = enc_total // seq_count
    scal, kvm, kvn = prepare(
        own, encoder_lengths.T, decoder_lengths.T, target_device.T, encoder_keys, encoder_values, owners, enc_cap
    )
    way, around = scal[WAY], scal[AROUND]
    ways = [
        (RING * i + min(j, KEY_HOPS), RING * i + min(j + 1, KEY_HOPS))
        for i in range(owners // RING)
        for j in range(KEY_HOPS + 1)
    ][1:]
    rest = [(max(j - KEY_HOPS, 0), j + 1 - KEY_HOPS) for j in range(KEY_HOPS - 1, RING // 2)]

    def queries_out(m, n):
        def run(xm, xn):
            xn = passed_along(xn, n)
            return xn, passed_along(xm, -m)

        return run

    def out_along(m, n, last):
        def run(scal, around, kvm, kvn, queries, context_grad):
            kvn = passed_along(kvn, -n)
            kvm = passed_along(kvm, m)
            xm, xn = pack(scal, exchanged(split(queries, context_grad), around >= 0), dec_cap)
            if last:
                xn, xm = lax.switch(around, [queries_out(*r) for r in rest], xm, xn)
            return kvn, kvm, xn, xm

        return run

    kvn, kvm, xn, xm = lax.switch(
        way,
        [out_along(*w, i % (KEY_HOPS + 1) == KEY_HOPS - 1) for i, w in enumerate(ways)],
        scal, around, kvm, kvn, queries, context_grad,
    )

    def queries_back(m, n):
        def run(ym, yn):
            yn = passed_along(yn, -n)
            return yn, passed_along(ym, m)

        return run

    yn, kvn = attend(1, scal, xn, kvn)
    ym, kvm = attend(0, scal, xm, kvm)
    yn, ym = lax.switch(around, [queries_back(*r) for r in rest], ym, yn)

    def back_along(m, n):
        def run(scal, around, kvm, kvn, ym, yn):
            kvn = passed_along(kvn, n)
            kvm = passed_along(kvm, -m)
            parts = merge_parts(scal, ym, yn, lax.axis_size("mp"))
            return kvn, kvm, *join(exchanged(parts, around >= 0))

        return run

    kvn, kvm, context, query_grad = lax.switch(
        way, [back_along(*w) for w in ways], scal, around, kvm, kvn, ym, yn
    )
    key_grad, value_grad = merge_keys(scal, kvm, kvn, enc_total)
    return (context, query_grad, key_grad, value_grad)


def solution(mesh):
    return jax.shard_map(
        local,
        mesh=mesh,
        in_specs=(
            P(("dp", "mp"), None),
            P("dp", "mp"),
            P("dp", "mp"),
            P(("dp", "mp"), None),
            P(),
            P(),
            P(),
        ),
        out_specs=(P(("dp", "mp"), None), P(("dp", "mp"), None), P("dp", "mp"), P("dp", "mp")),
        check_vma=False,
    )
```

profile of v0, /device:TPU:1, one launch (start us, length us, event | category | flops | bytes accessed | tf_op | source)
XLA Modules:
  0.0 149.0 jit_solution(3010438921841794882)
XLA Ops:
  0.6 0.0 copy-start.3
  0.6 0.0 copy-start.4
  0.7 0.0 copy-start.2
  0.7 0.7 copy-done.3
  1.3 0.0 copy-done.4
  1.3 0.0 copy-done.2
  1.3 0.0 copy-start
  1.4 1.1 copy-done
  2.4 0.0 copy-start.1
  2.4 1.1 copy-done.1
  3.5 0.0 copy-start.5
  3.5 0.0 copy-start.6
  3.5 1.9 %shard_map.102 = (s32[16]{0:T(128)S(1)}, bf16[2,576,256]{2,1,0:T(8,128)(2,1)S(1)}, bf16[2,576,256]{2,1,0:T(8,128)(2,1)S(1)}) custom-call(s32[1]{0:T(128)} %bitcast.own_ref, s32[2,64]{1,0:T(2,128)S(1)} %bitcast.6, s32[2,64]{1,0:T(2,128)S(1)} %bitcast.7, s32[2,64]{1,0:T(2,128)S(1)} %bitcast.8, bf16[1152,256]{1,0:T(8,128)(2,1)S(1)} %copy-done, ...), custom_call_target="tpu_custom_call" | custom-call | tf_op jit(solution)/shard_map/pallas_call | solution.py:90
  5.4 0.6 fusion
  7.3 0.0 copy-done.5
  7.3 0.0 copy-done.6
  7.3 64.9 %conditional.29 = (bf16[2,576,256]{2,1,0:T(8,128)(2,1)}, bf16[2,576,256]{2,1,0:T(8,128)(2,1)}, bf16[2,512,256]{2,1,0:T(8,128)(2,1)}, bf16[2,512,256]{2,1,0:T(8,128)(2,1)}) conditional(s32[]{:T(128)} %bitcast.4, (bf16[2,576,256]{2,1,0:T(8,128)(2,1)S(1)}, bf16[2,576,256]{2,1,0:T(8,128)(2,1)S(1)}, s32[]{:T(128)}, ...), branch_computations={%region_0.0_spmd, %region_3.0_spmd, %region_13.0_spmd, %region_16.... | conditional | flops 3 | bytes 15204622 | solution.py:304
  7.4 13.3 %collective-permute-start.47 = (bf16[2,576,256]{2,1,0:T(8,128)(2,1)S(1)}, bf16[2,576,256]{2,1,0:T(8,128)(2,1)}, u32[]{:S(2)}, u32[]{:S(2)}) collective-permute-start(bf16[2,576,256]{2,1,0:T(8,128)(2,1)S(1)} %get-tuple-element.610), channel_id=1, source_target_pairs={{0,240},{8,248},{16,256},{24,264},{32,272},{40,280},{48,288},{56,2... | collective-permute-start | bytes 1769480 | tf_op jit(solution)/shard_map/cond/branch_7_fun/ppermute | solution.py:30
  20.7 1.9 %collective-permute-start.48 = (bf16[2,576,256]{2,1,0:T(8,128)(2,1)S(1)}, bf16[2,576,256]{2,1,0:T(8,128)(2,1)}, u32[]{:S(2)}, u32[]{:S(2)}) collective-permute-start(bf16[2,576,256]{2,1,0:T(8,128)(2,1)S(1)} %get-tuple-element.611), channel_id=1, source_target_pairs={{0,272},{8,280},{16,288},{24,296},{32,304},{40,312},{48,320},{56,3... | collective-permute-start | bytes 1769480 | tf_op jit(solution)/shard_map/cond/branch_7_fun/ppermute | solution.py:30
  23.9 0.1 branch_7_fun.4
  24.0 20.8 %conditional.9 = (bf16[8,2,128,256]{3,2,1,0:T(8,128)(2,1)S(1)}) conditional(s32[]{:T(128)} %convert_element_type.51, bf16[8,2,128,256]{3,2,1,0:T(8,128)(2,1)S(1)} %branch_7_fun.4, bf16[8,2,128,256]{3,2,1,0:T(8,128)(2,1)S(1)} %branch_7_fun.4), branch_computations={%region_36.0_spmd, %region_37.0_spmd} | conditional | bytes 4194312 | solution.py:256
  24.0 0.1 copy.220
  24.1 20.7 %all_to_all.95 = bf16[8,2,128,256]{3,2,1,0:T(8,128)(2,1)S(1)} all-to-all(bf16[8,2,128,256]{3,2,1,0:T(8,128)(2,1)S(1)} %copy.220), channel_id=1, replica_groups=mesh['dp'=64,'mp'=8] {'mp'}, dimensions={0} | all-to-all | bytes 2097152 | tf_op jit(solution)/shard_map/cond/branch_7_fun/cond/branch_1_fun/all_to_all | solution.py:254
  44.8 2.8 %branch_7_fun.5 = (bf16[2,512,256]{2,1,0:T(8,128)(2,1)}, bf16[2,512,256]{2,1,0:T(8,128)(2,1)}) custom-call(s32[16]{0:T(128)S(1)} %get-tuple-element.613.scal, bf16[8,2,128,256]{3,2,1,0:T(8,128)(2,1)S(1)} %get-tuple-element.969.in_ref), custom_call_target="tpu_custom_call" | custom-call | tf_op jit(solution)/shard_map/cond/branch_7_fun/pallas_call | solution.py:151
  47.6 24.6 %conditional.10 = ((bf16[2,512,256]{2,1,0:T(8,128)(2,1)}, bf16[2,512,256]{2,1,0:T(8,128)(2,1)})) conditional(s32[]{:T(128)} %clamp.17, (bf16[2,512,256]{2,1,0:T(8,128)(2,1)}, bf16[2,512,256]{2,1,0:T(8,128)(2,1)}) %tuple.291, (bf16[2,512,256]{2,1,0:T(8,128)(2,1)}, bf16[2,512,256]{2,1,0:T(8,128)(2,1)}) %tuple.291, ...), branch_computations={%region_38.0_spmd, %region_39.0_spmd, %region_40.0_spmd, %region_4... | conditional | bytes 6291560 | solution.py:299
  47.6 1.9 %collective-permute-start.37 = (bf16[2,512,256]{2,1,0:T(8,128)(2,1)}, bf16[2,512,256]{2,1,0:T(8,128)(2,1)S(1)}, u32[]{:S(2)}, u32[]{:S(2)}) collective-permute-start(bf16[2,512,256]{2,1,0:T(8,128)(2,1)} %get-tuple-element.600), channel_id=1, source_target_pairs={{0,16},{8,24},{16,32},{24,40},{32,48},{40,56},{48,64},{56,72},{64,... | collective-permute-start | bytes 1572872 | tf_op jit(solution)/shard_map/cond/branch_7_fun/cond/branch_2_fun/ppermute | solution.py:30
  49.5 7.5 %collective-permute-start.38 = (bf16[2,512,256]{2,1,0:T(8,128)(2,1)}, bf16[2,512,256]{2,1,0:T(8,128)(2,1)S(1)}, u32[]{:S(2)}, u32[]{:S(2)}) collective-permute-start(bf16[2,512,256]{2,1,0:T(8,128)(2,1)} %get-tuple-element.601), channel_id=1, source_target_pairs={{0,504},{8,0},{16,8},{24,16},{32,24},{40,32},{48,40},{56,48},{64,5... | collective-permute-start | bytes 1572872 | tf_op jit(solution)/shard_map/cond/branch_7_fun/cond/branch_2_fun/ppermute | solution.py:30
  57.0 13.6 %collective-permute-done.37 = bf16[2,512,256]{2,1,0:T(8,128)(2,1)S(1)} collective-permute-done((bf16[2,512,256]{2,1,0:T(8,128)(2,1)}, bf16[2,512,256]{2,1,0:T(8,128)(2,1)S(1)}, u32[]{:S(2)}, u32[]{:S(2)}) %collective-permute-start.37) | collective-permute-done | bytes 524320 | tf_op jit(solution)/shard_map/cond/branch_7_fun/cond/branch_2_fun/ppermute | solution.py:30
  70.6 0.8 copy.59
  71.4 0.0 collective-permute-done.38
  71.4 0.8 copy.60
  72.2 0.0 collective-permute-done.47
  72.2 0.0 collective-permute-done.48
  72.2 4.0 %shard_map.103 = (bf16[2,512,256]{2,1,0:T(8,128)(2,1)S(1)}, bf16[2,576,256]{2,1,0:T(8,128)(2,1)S(1)}) custom-call(s32[16]{0:T(128)S(1)} %get-tuple-element.781.scal, bf16[2,512,256]{2,1,0:T(8,128)(2,1)} %get-tuple-element.784.x_ref, bf16[2,576,256]{2,1,0:T(8,128)(2,1)} %get-tuple-element.785.kv_ref), custom_call_target="tpu_custom_call" | custom-call | flops 905969664 | bytes 3145728 | tf_op jit(solution)/shard_map/pallas_call | solution.py:238
  76.2 4.0 %shard_map.104 = (bf16[2,512,256]{2,1,0:T(8,128)(2,1)S(1)}, bf16[2,576,256]{2,1,0:T(8,128)(2,1)S(1)}) custom-call(s32[16]{0:T(128)S(1)} %get-tuple-element.781.scal, bf16[2,512,256]{2,1,0:T(8,128)(2,1)} %get-tuple-element.787.x_ref, bf16[2,576,256]{2,1,0:T(8,128)(2,1)} %get-tuple-element.788.kv_ref), custom_call_target="tpu_custom_call" | custom-call | flops 905969664 | bytes 3145728 | tf_op jit(solution)/shard_map/pallas_call | solution.py:238
  80.1 27.8 %conditional.30 = ((bf16[2,512,256]{2,1,0:T(8,128)(2,1)S(1)}, bf16[2,512,256]{2,1,0:T(8,128)(2,1)S(1)})) conditional(s32[]{:T(128)} %clamp.24, (bf16[2,512,256]{2,1,0:T(8,128)(2,1)S(1)}, bf16[2,512,256]{2,1,0:T(8,128)(2,1)S(1)}) %tuple.364, (bf16[2,512,256]{2,1,0:T(8,128)(2,1)S(1)}, ...), branch_computations={%region_61.0_spmd, %region_62.0_spmd, %region_63.0_spmd, %region_6... | conditional | bytes 6291560 | solution.py:319
  80.2 4.2 %collective-permute-start.67 = (bf16[2,512,256]{2,1,0:T(8,128)(2,1)S(1)}, bf16[2,512,256]{2,1,0:T(8,128)(2,1)S(1)}, u32[]{:S(2)}, u32[]{:S(2)}) collective-permute-start(bf16[2,512,256]{2,1,0:T(8,128)(2,1)S(1)} %get-tuple-element.660), channel_id=1, source_target_pairs={{0,496},{8,504},{16,0},{24,8},{32,16},{40,24},{48,32},{56,40},{64,... | collective-permute-start | bytes 1572872 | tf_op jit(solution)/shard_map/cond/branch_2_fun/ppermute | solution.py:30
  84.4 11.0 %collective-permute-start.68 = (bf16[2,512,256]{2,1,0:T(8,128)(2,1)S(1)}, bf16[2,512,256]{2,1,0:T(8,128)(2,1)S(1)}, u32[]{:S(2)}, u32[]{:S(2)}) collective-permute-start(bf16[2,512,256]{2,1,0:T(8,128)(2,1)S(1)} %get-tuple-element.661), channel_id=1, source_target_pairs={{0,8},{8,16},{16,24},{24,32},{32,40},{40,48},{48,56},{56,64},{64,7... | collective-permute-start | bytes 1572872 | tf_op jit(solution)/shard_map/cond/branch_2_fun/ppermute | solution.py:30
  95.4 0.0 collective-permute-done.67
  95.4 12.5 %collective-permute-done.68 = bf16[2,512,256]{2,1,0:T(8,128)(2,1)S(1)} collective-permute-done((bf16[2,512,256]{2,1,0:T(8,128)(2,1)S(1)}, bf16[2,512,256]{2,1,0:T(8,128)(2,1)S(1)}, u32[]{:S(2)}, u32[]{:S(2)}) %collective-permute-start.68) | collective-permute-done | bytes 524320 | tf_op jit(solution)/shard_map/cond/branch_2_fun/ppermute | solution.py:30
  107.9 37.7 %conditional.31 = (bf16[2,576,256]{2,1,0:T(8,128)(2,1)}, bf16[2,576,256]{2,1,0:T(8,128)(2,1)}, bf16[128,2048]{1,0:T(8,128)(2,1)}, bf16[128,2048]{1,0:T(8,128)(2,1)}) conditional(s32[]{:T(128)} %bitcast.4, (bf16[2,576,256]{2,1,0:T(8,128)(2,1)S(1)}, bf16[2,576,256]{2,1,0:T(8,128)(2,1)S(1)}, s32[]{:T(128)}, ...), branch_computations={%region_68.0_spmd, %region_71.0_spmd, %region_74.0_spmd, %region_7... | conditional | flops 2 | bytes 8913030 | solution.py:330
  108.0 1.9 %collective-permute-start.91 = (bf16[2,576,256]{2,1,0:T(8,128)(2,1)S(1)}, bf16[2,576,256]{2,1,0:T(8,128)(2,1)}, u32[]{:S(2)}, u32[]{:S(2)}) collective-permute-start(bf16[2,576,256]{2,1,0:T(8,128)(2,1)S(1)} %get-tuple-element.726), channel_id=1, source_target_pairs={{0,272},{8,280},{16,288},{24,296},{32,304},{40,312},{48,320},{56,3... | collective-permute-start | bytes 1769480 | tf_op jit(solution)/shard_map/cond/branch_7_fun/ppermute | solution.py:30
  109.9 6.4 %collective-permute-start.92 = (bf16[2,576,256]{2,1,0:T(8,128)(2,1)S(1)}, bf16[2,576,256]{2,1,0:T(8,128)(2,1)}, u32[]{:S(2)}, u32[]{:S(2)}) collective-permute-start(bf16[2,576,256]{2,1,0:T(8,128)(2,1)S(1)} %get-tuple-element.727), channel_id=1, source_target_pairs={{0,240},{8,248},{16,256},{24,264},{32,272},{40,280},{48,288},{56,2... | collective-permute-start | bytes 1769480 | tf_op jit(solution)/shard_map/cond/branch_7_fun/ppermute | solution.py:30
  116.9 2.5 %branch_7_fun.6 = bf16[8,2,128,256]{3,2,1,0:T(8,128)(2,1)S(1)} custom-call(s32[16]{0:T(128)S(1)} %get-tuple-element.729.scal, bf16[2,512,256]{2,1,0:T(8,128)(2,1)S(1)} %get-tuple-element.730.a_ref, bf16[2,512,256]{2,1,0:T(8,128)(2,1)S(1)} %get-tuple-element.731.b_ref), custom_call_target="tpu_custom_call" | custom-call | tf_op jit(solution)/shard_map/cond/branch_7_fun/pallas_call | solution.py:181
  119.5 25.1 %conditional.22 = (bf16[8,2,128,256]{3,2,1,0:T(8,128)(2,1)S(1)}) conditional(s32[]{:T(128)} %convert_element_type.62, bf16[8,2,128,256]{3,2,1,0:T(8,128)(2,1)S(1)} %branch_7_fun.6, bf16[8,2,128,256]{3,2,1,0:T(8,128)(2,1)S(1)} %branch_7_fun.6), branch_computations={%region_90.0_spmd, %region_91.0_spmd} | conditional | bytes 4194312 | solution.py:256
  119.5 0.1 copy.231
  119.6 24.9 %all_to_all.106 = bf16[8,2,128,256]{3,2,1,0:T(8,128)(2,1)S(1)} all-to-all(bf16[8,2,128,256]{3,2,1,0:T(8,128)(2,1)S(1)} %copy.231), channel_id=1, replica_groups=mesh['dp'=64,'mp'=8] {'mp'}, dimensions={0} | all-to-all | bytes 2097152 | tf_op jit(solution)/shard_map/cond/branch_7_fun/cond/branch_1_fun/all_to_all | solution.py:254
  144.5 1.1 branch_7_fun.7
  145.6 0.0 collective-permute-done.91
  145.6 0.0 collective-permute-done.92
  145.6 3.4 %shard_map.105 = (bf16[1152,256]{1,0:T(8,128)(2,1)}, bf16[1152,256]{1,0:T(8,128)(2,1)}) custom-call(s32[16]{0:T(128)S(1)} %get-tuple-element.781.scal, bf16[2,576,256]{2,1,0:T(8,128)(2,1)} %get-tuple-element.796.a_ref, bf16[2,576,256]{2,1,0:T(8,128)(2,1)} %get-tuple-element.797.b_ref), custom_call_target="tpu_custom_call" | custom-call | tf_op jit(solution)/shard_map/pallas_call | solution.py:196
  (2 shorter events, 0.1 us)
Async XLA Ops:
  0.6 0.7 copy-start.3
  0.6 0.7 copy-start.4
  0.7 0.7 copy-start.2
  1.3 1.1 copy-start
  2.4 1.1 copy-start.1
  3.5 3.8 %copy-start.5 = (bf16[128,2048]{1,0:T(8,128)(2,1)S(1)}, bf16[128,2048]{1,0:T(8,128)(2,1)}, u32[]{:S(2)}) copy-start(bf16[128,2048]{1,0:T(8,128)(2,1)} %param.108) | copy-start | bytes 1572868
  3.5 3.8 %copy-start.6 = (bf16[128,2048]{1,0:T(8,128)(2,1)S(1)}, bf16[128,2048]{1,0:T(8,128)(2,1)}, u32[]{:S(2)}) copy-start(bf16[128,2048]{1,0:T(8,128)(2,1)} %param.111) | copy-start | bytes 1572868
  7.4 64.8 %collective-permute-start.47 = (bf16[2,576,256]{2,1,0:T(8,128)(2,1)S(1)}, bf16[2,576,256]{2,1,0:T(8,128)(2,1)}, u32[]{:S(2)}, u32[]{:S(2)}) collective-permute-start(bf16[2,576,256]{2,1,0:T(8,128)(2,1)S(1)} %get-tuple-element.610), channel_id=1, source_target_pairs={{0,240},{8,248},{16,256},{24,264},{32,272},{40,280},{48,288},{56,2... | collective-permute-start | bytes 1769480 | tf_op jit(solution)/shard_map/cond/branch_7_fun/ppermute | solution.py:30
  20.7 51.5 %collective-permute-start.48 = (bf16[2,576,256]{2,1,0:T(8,128)(2,1)S(1)}, bf16[2,576,256]{2,1,0:T(8,128)(2,1)}, u32[]{:S(2)}, u32[]{:S(2)}) collective-permute-start(bf16[2,576,256]{2,1,0:T(8,128)(2,1)S(1)} %get-tuple-element.611), channel_id=1, source_target_pairs={{0,272},{8,280},{16,288},{24,296},{32,304},{40,312},{48,320},{56,3... | collective-permute-start | bytes 1769480 | tf_op jit(solution)/shard_map/cond/branch_7_fun/ppermute | solution.py:30
  47.6 23.0 %collective-permute-start.37 = (bf16[2,512,256]{2,1,0:T(8,128)(2,1)}, bf16[2,512,256]{2,1,0:T(8,128)(2,1)S(1)}, u32[]{:S(2)}, u32[]{:S(2)}) collective-permute-start(bf16[2,512,256]{2,1,0:T(8,128)(2,1)} %get-tuple-element.600), channel_id=1, source_target_pairs={{0,16},{8,24},{16,32},{24,40},{32,48},{40,56},{48,64},{56,72},{64,... | collective-permute-start | bytes 1572872 | tf_op jit(solution)/shard_map/cond/branch_7_fun/cond/branch_2_fun/ppermute | solution.py:30
  49.5 21.9 %collective-permute-start.38 = (bf16[2,512,256]{2,1,0:T(8,128)(2,1)}, bf16[2,512,256]{2,1,0:T(8,128)(2,1)S(1)}, u32[]{:S(2)}, u32[]{:S(2)}) collective-permute-start(bf16[2,512,256]{2,1,0:T(8,128)(2,1)} %get-tuple-element.601), channel_id=1, source_target_pairs={{0,504},{8,0},{16,8},{24,16},{32,24},{40,32},{48,40},{56,48},{64,5... | collective-permute-start | bytes 1572872 | tf_op jit(solution)/shard_map/cond/branch_7_fun/cond/branch_2_fun/ppermute | solution.py:30
  80.2 15.2 %collective-permute-start.67 = (bf16[2,512,256]{2,1,0:T(8,128)(2,1)S(1)}, bf16[2,512,256]{2,1,0:T(8,128)(2,1)S(1)}, u32[]{:S(2)}, u32[]{:S(2)}) collective-permute-start(bf16[2,512,256]{2,1,0:T(8,128)(2,1)S(1)} %get-tuple-element.660), channel_id=1, source_target_pairs={{0,496},{8,504},{16,0},{24,8},{32,16},{40,24},{48,32},{56,40},{64,... | collective-permute-start | bytes 1572872 | tf_op jit(solution)/shard_map/cond/branch_2_fun/ppermute | solution.py:30
  84.4 23.5 %collective-permute-start.68 = (bf16[2,512,256]{2,1,0:T(8,128)(2,1)S(1)}, bf16[2,512,256]{2,1,0:T(8,128)(2,1)S(1)}, u32[]{:S(2)}, u32[]{:S(2)}) collective-permute-start(bf16[2,512,256]{2,1,0:T(8,128)(2,1)S(1)} %get-tuple-element.661), channel_id=1, source_target_pairs={{0,8},{8,16},{16,24},{24,32},{32,40},{40,48},{48,56},{56,64},{64,7... | collective-permute-start | bytes 1572872 | tf_op jit(solution)/shard_map/cond/branch_2_fun/ppermute | solution.py:30
  108.0 37.6 %collective-permute-start.91 = (bf16[2,576,256]{2,1,0:T(8,128)(2,1)S(1)}, bf16[2,576,256]{2,1,0:T(8,128)(2,1)}, u32[]{:S(2)}, u32[]{:S(2)}) collective-permute-start(bf16[2,576,256]{2,1,0:T(8,128)(2,1)S(1)} %get-tuple-element.726), channel_id=1, source_target_pairs={{0,272},{8,280},{16,288},{24,296},{32,304},{40,312},{48,320},{56,3... | collective-permute-start | bytes 1769480 | tf_op jit(solution)/shard_map/cond/branch_7_fun/ppermute | solution.py:30
  109.9 35.7 %collective-permute-start.92 = (bf16[2,576,256]{2,1,0:T(8,128)(2,1)S(1)}, bf16[2,576,256]{2,1,0:T(8,128)(2,1)}, u32[]{:S(2)}, u32[]{:S(2)}) collective-permute-start(bf16[2,576,256]{2,1,0:T(8,128)(2,1)S(1)} %get-tuple-element.727), channel_id=1, source_target_pairs={{0,240},{8,248},{16,256},{24,264},{32,272},{40,280},{48,288},{56,2... | collective-permute-start | bytes 1769480 | tf_op jit(solution)/shard_map/cond/branch_7_fun/ppermute | solution.py:30
where the time goes:
time: 152 us; the launch traced here: 149 us
  starting transfers between devices  48.1 us (32%)
  blocking collectives  45.6 us (30%)
  waiting for transfers between devices  26.1 us (17%)
  Pallas kernels  19.7 us (13%)
  local copies, waits for them, and re-layouts  5.24 us (3%)
  loops' own time  2.23 us (1%)
  between operations  2.02 us (1%)
    ppermute x8, starting transfers between devices, passed_along(): lax.ppermute(block, 'dp', [(i, (i + distance) % owners) for i in range(ow...  48.1 us
    all_to_all x2, blocking collectives, swap(): return lax.all_to_all(parts, 'mp', split_axis=0, concat_axis=0, tiled=True)  45.6 us
    ppermute x8, waiting for transfers between devices, passed_along(): lax.ppermute(block, 'dp', [(i, (i + distance) % owners) for i in range(ow...  26.1 us
    pallas_call x2, Pallas kernels, attend(): pl.pallas_call(functools.partial(attend_kernel, n), grid=(cap // ROWS,),...  7.93 us
    pallas_call x1, Pallas kernels, merge_keys(): pl.pallas_call(merge_keys_kernel, in_specs=[SMEM, pl.BlockSpec(), pl.Bloc...  3.39 us
  transfers between devices with their start and end apart: 8, of which 2 were waited for; matrix products, arithmetic and copies ran while one was open for 1% of the time, Pallas kernels for 4%

commit v1 on v0

--- a/solution.py
+++ b/solution.py
@@ -17,6 +17,7 @@
 TN = (((0,), (0,)), ((), ()))
 WAY, AROUND, COL, DEC_LEN, ENC_LEN, KEY_LEN, QUERY_LEN = 0, 1, 2, 4, 6, 8, 10
 PARAMS = pltpu.CompilerParams(vmem_limit_bytes=32 * 2**20)
+WIDE = pltpu.CompilerParams(vmem_limit_bytes=60 * 2**20)
 
 
 def dot(a, b, dims=(((1,), (0,)), ((), ()))):
@@ -47,17 +48,15 @@
         n_ref[c] = jnp.where(m == 0, second, first)
 
 
-def packed(m, len0, len1, a, b, total):
-    cap = a.shape[0]
-    first = jnp.where(m == 0, a, b)
-    second = jnp.where(m == 0, b, a)
-    live = lax.broadcasted_iota(jnp.int32, (cap, 1), 0) < len0
-    first = jnp.where(live, first, jnp.zeros_like(first)).astype(jnp.float32)
-    moved = dot(one_hot((total, cap), -len0, len1), second)
-    return jnp.concatenate([moved[:cap] + first, moved[cap:]], axis=0).astype(a.dtype)
-
-
-def prepare_kernel(owners, own_ref, enc_ref, dec_ref, target_ref, k_ref, v_ref, out_ref, kvm_ref, kvn_ref):
+def prepare_kernel(
+    owners, own_ref, enc_ref, dec_ref, target_ref, k_hbm, v_hbm, out_ref, kvm_ref, kvn_ref, k_ref, v_ref, sems
+):
+    copies = [
+        pltpu.make_async_copy(k_hbm, k_ref, sems.at[0]),
+        pltpu.make_async_copy(v_hbm, v_ref, sems.at[1]),
+    ]
+    for copy in copies:
+        copy.start()
     own = own_ref[0]
     shift0 = lax.rem(target_ref[0, 0], owners)
     m = jnp.where(lax.rem(shift0, RING) < RING // 2, 0, 1)
@@ -82,6 +81,8 @@
         out_ref[QUERY_LEN + n] = dec_ref[col, wrapped(own + sign * (h + n - hops))]
     for n in range(QUERY_LEN + 2, out_ref.shape[0]):
         out_ref[n] = 0
+    for copy in copies:
+        copy.wait()
     unpacked(m, enc_ref[0, own], enc_ref[1, own], (k_ref[...], v_ref[...]), kvm_ref, kvn_ref)
 
 
@@ -89,10 +90,11 @@
     slot = jax.ShapeDtypeStruct((2, cap, HEAD_DIM), keys.dtype)
     return pl.pallas_call(
         functools.partial(prepare_kernel, owners),
-        in_specs=[SMEM] * 4 + [pl.BlockSpec()] * 2,
+        in_specs=[SMEM] * 4 + [pl.BlockSpec(memory_space=pl.ANY)] * 2,
         out_specs=[SMEM] + [pl.BlockSpec()] * 2,
         out_shape=[jax.ShapeDtypeStruct((16,), jnp.int32), slot, slot],
-        compiler_params=PARAMS,
+        scratch_shapes=[pltpu.VMEM(keys.shape, keys.dtype)] * 2 + [pltpu.SemaphoreType.DMA((2,))],
+        compiler_params=WIDE,
     )(own, enc, dec, target, keys, values)
 
 
@@ -186,67 +188,96 @@
     )(scal, a, b)
 
 
-def merge_keys_kernel(scal, a_ref, b_ref, *outs):
-    for c, out_ref in enumerate(outs):
-        rows = packed(scal[COL], scal[ENC_LEN], scal[ENC_LEN + 1], a_ref[c], b_ref[c], out_ref.shape[0])
-        out_ref[...] = rows
+def merge_keys_kernel(scal, a_hbm, b_hbm, dk_hbm, dv_hbm, a_ref, b_ref, out_ref, sems):
+    count, cap, _ = a_ref.shape
+    total = out_ref.shape[1]
+    ins = [
+        [pltpu.make_async_copy(src.at[c], dst.at[c], sems.at[i, c]) for i, (src, dst) in enumerate(pairs)]
+        for c, pairs in enumerate([((a_hbm, a_ref), (b_hbm, b_ref))] * count)
+    ]
+    outs = [pltpu.make_async_copy(out_ref.at[c], dst, sems.at[2, c]) for c, dst in enumerate((dk_hbm, dv_hbm))]
+    for copies in ins:
+        for copy in copies:
+            copy.start()
+    m, len0, len1 = scal[COL], scal[ENC_LEN], scal[ENC_LEN + 1]
+    low = cap // 2
+    pick = one_hot((total - low, cap), low - len0, len1)
+    live = lax.broadcasted_iota(jnp.int32, (cap, 1), 0) < len0
+    for c in range(count):
+        for copy in ins[c]:
+            copy.wait()
+        first = jnp.where(m == 0, a_ref[c], b_ref[c])
+        second = jnp.where(m == 0, b_ref[c], a_ref[c])
+        first = jnp.where(live, first, jnp.zeros_like(first)).astype(jnp.float32)
+        moved = dot(pick, second)
+        out_ref[c, :low] = first[:low].astype(out_ref.dtype)
+        out_ref[c, low:cap] = (moved[: cap - low] + first[low:]).astype(out_ref.dtype)
+        out_ref[c, cap:] = moved[cap - low :].astype(out_ref.dtype)
+        outs[c].start()
+    for copy in outs:
+        copy.wait()
 
 
 def merge_keys(scal, a, b, total):
+    hbm = pl.BlockSpec(memory_space=pl.ANY)
     return pl.pallas_call(
         merge_keys_kernel,
-        in_specs=[SMEM, pl.BlockSpec(), pl.BlockSpec()],
+        in_specs=[SMEM, hbm, hbm],
+        out_specs=[hbm, hbm],
         out_shape=[jax.ShapeDtypeStruct((total, HEAD_DIM), a.dtype)] * a.shape[0],
-        compiler_params=PARAMS,
+        scratch_shapes=[
+            pltpu.VMEM(a.shape, a.dtype),
+            pltpu.VMEM(b.shape, b.dtype),
+            pltpu.VMEM((a.shape[0], total, HEAD_DIM), a.dtype),
+            pltpu.SemaphoreType.DMA((3, a.shape[0])),
+        ],
+        compiler_params=WIDE,
     )(scal, a, b)
 
 
-def attend_kernel(n, scal, x_ref, kv_ref, y_ref, dkv_ref, acc_ref):
-    step = pl.program_id(0)
-    rows = x_ref.shape[1]
-    valid = lax.broadcasted_iota(jnp.int32, (rows, 1), 0) + step * rows < scal[QUERY_LEN + n]
-    q, g, keys, values = x_ref[0], x_ref[1], kv_ref[0], kv_ref[1]
+def attend_rows(q, g, keys, values, key_len, valid):
     scores = dot(q, keys, NT) * SCALING
     col = lax.broadcasted_iota(jnp.int32, (1, scores.shape[1]), 1)
-    scores = jnp.where(col < scal[KEY_LEN + n], scores, -1e30)
+    scores = jnp.where(col < key_len, scores, -1e30)
     raised = jnp.exp(scores - jnp.max(scores, axis=1, keepdims=True))
     probs = raised * (1.0 / jnp.sum(raised, axis=1, keepdims=True))
     probs_b = probs.astype(jnp.bfloat16)
     prob_grad = dot(g, values, NT)
     row_dot = jnp.sum(probs * prob_grad, axis=1, keepdims=True)
     score_grad = (probs * (prob_grad - row_dot)).astype(jnp.bfloat16)
-    y_ref[0] = jnp.where(valid, dot(probs_b, values), 0.0).astype(y_ref.dtype)
-    y_ref[1] = jnp.where(valid, dot(score_grad, keys) * SCALING, 0.0).astype(y_ref.dtype)
-
-    @pl.when(step == 0)
-    def _():
-        acc_ref[...] = jnp.zeros_like(acc_ref)
-
-    acc_ref[0] += dot(score_grad, q, TN)
-    acc_ref[1] += dot(probs_b, g, TN)
-
-    @pl.when(step == pl.num_programs(0) - 1)
-    def _():
-        dkv_ref[0] = (acc_ref[0] * SCALING).astype(dkv_ref.dtype)
-        dkv_ref[1] = acc_ref[1].astype(dkv_ref.dtype)
-
-
-def attend(n, scal, x, kv):
-    cap, keys = x.shape[1], kv.shape[1]
-    blocks = pl.BlockSpec((2, ROWS, HEAD_DIM), lambda i: (0, i, 0))
-    whole = pl.BlockSpec(kv.shape, lambda i: (0, 0, 0))
-    return pl.pallas_call(
-        functools.partial(attend_kernel, n),
-        grid=(cap // ROWS,),
-        in_specs=[SMEM, blocks, whole],
-        out_specs=[blocks, whole],
-        out_shape=[jax.ShapeDtypeStruct(x.shape, x.dtype), jax.ShapeDtypeStruct(kv.shape, kv.dtype)],
-        scratch_shapes=[pltpu.VMEM(kv.shape, jnp.float32)],
+    context = jnp.where(valid, dot(probs_b, values), 0.0).astype(jnp.bfloat16)
+    query_grad = jnp.where(valid, dot(score_grad, keys) * SCALING, 0.0).astype(jnp.bfloat16)
+    return context, query_grad, probs_b, score_grad
+
+
+def attend_kernel(scal, xm_ref, xn_ref, kvm_ref, kvn_ref, ym_ref, yn_ref, dkvm_ref, dkvn_ref):
+    columns = ((xm_ref, kvm_ref, ym_ref, dkvm_ref), (xn_ref, kvn_ref, yn_ref, dkvn_ref))
+    for n, (x_ref, kv_ref, y_ref, dkv_ref) in enumerate(columns):
+        probs, score_grads = [], []
+        for base in range(0, x_ref.shape[1], ROWS):
+            at = slice(base, base + ROWS)
+            valid = lax.broadcasted_iota(jnp.int32, (ROWS, 1), 0) + base < scal[QUERY_LEN + n]
+            y_ref[0, at], y_ref[1, at], probs_b, score_grad = attend_rows(
+                x_ref[0, at], x_ref[1, at], kv_ref[0], kv_ref[1], scal[KEY_LEN + n], valid
+            )
+            probs.append(probs_b)
+            score_grads.append(score_grad)
+        key_grad = dot(jnp.concatenate(score_grads), x_ref[0], TN) * SCALING
+        dkv_ref[0] = key_grad.astype(dkv_ref.dtype)
+        dkv_ref[1] = dot(jnp.concatenate(probs), x_ref[1], TN).astype(dkv_ref.dtype)
+
+
+def attend(scal, xm, xn, kvm, kvn):
+    cap, keys = xm.shape[1], kvm.shape[1]
+    return pl.pallas_call(
+        attend_kernel,
+        in_specs=[SMEM] + [pl.BlockSpec()] * 4,
+        out_shape=[jax.ShapeDtypeStruct(a.shape, a.dtype) for a in (xm, xn, kvm, kvn)],
         compiler_params=PARAMS,
         cost_estimate=pl.CostEstimate(
-            flops=12 * cap * keys * HEAD_DIM, bytes_accessed=3 * 2**20, transcendentals=cap * keys
+            flops=24 * cap * keys * HEAD_DIM, bytes_accessed=5 * 2**20, transcendentals=2 * cap * keys
         ),
-    )(scal, x, kv)
+    )(scal, xm, xn, kvm, kvn)
 
 
 def exchanged(parts, flag):
@@ -314,8 +345,7 @@
 
         return run
 
-    yn, kvn = attend(1, scal, xn, kvn)
-    ym, kvm = attend(0, scal, xm, kvm)
+    ym, yn, kvm, kvn = attend(scal, xm, xn, kvm, kvn)
     yn, ym = lax.switch(around, [queries_back(*r) for r in rest], ym, yn)
 
     def back_along(m, n):

time: 152 us -> 188 us (1.24); the launches traced: 149 us -> 187 us
  waiting for transfers between devices: 26.1 us -> 65.5 us
  starting transfers between devices: 48.1 us -> 56.7 us
  blocking collectives: 45.6 us -> 39.7 us
  local copies, waits for them, and re-layouts: 5.24 us -> 2.43 us
    ppermute x8, waiting for transfers between devices: 26.1 us -> 65.5 us  [passed_along(): lax.ppermute(block, 'dp', [(i, (i + distance) % owners) for i in range(ow...]
    ppermute x8, starting transfers between devices: 48.1 us -> 56.7 us  [passed_along(): lax.ppermute(block, 'dp', [(i, (i + distance) % owners) for i in range(ow...]
    all_to_all x2, blocking collectives: 45.6 us -> 39.7 us  [swap(): return lax.all_to_all(parts, 'mp', split_axis=0, concat_axis=0, tiled=True)]
    unnamed x14 -> x4, local copies, waits for them, and re-layouts: 2.82 us -> 0.01 us
    pallas_call x3 -> x2, Pallas kernels: 11.3 us -> 9.25 us  [the longest x1 5.12 us: attend(): pl.pallas_call(attend_kernel, in_specs=[SMEM] + [pl.BlockSpec()] * 4, out...]
  transfers between devices with their start and end apart: 8 -> 8, of which waited for: 2 -> 4; matrix products, arithmetic and copies ran while one was open for 1% -> 1% of each run, Pallas kernels for 4% -> 3%
where the time goes in v1:
time: 188 us; the launch traced here: 187 us
  waiting for transfers between devices  65.5 us (35%)
  starting transfers between devices  56.7 us (30%)
  blocking collectives  39.7 us (21%)
  Pallas kernels  18.8 us (10%)
  local copies, waits for them, and re-layouts  2.43 us (1%)
  loops' own time  2.2 us (1%)
  between operations  2.16 us (1%)
    ppermute x8, waiting for transfers between devices, passed_along(): lax.ppermute(block, 'dp', [(i, (i + distance) % owners) for i in range(ow...  65.5 us
    ppermute x8, starting transfers between devices, passed_along(): lax.ppermute(block, 'dp', [(i, (i + distance) % owners) for i in range(ow...  56.7 us
    all_to_all x2, blocking collectives, swap(): return lax.all_to_all(parts, 'mp', split_axis=0, concat_axis=0, tiled=True)  39.7 us
    pallas_call x1, Pallas kernels, attend(): pl.pallas_call(attend_kernel, in_specs=[SMEM] + [pl.BlockSpec()] * 4, out...  5.12 us
    pallas_call x1, Pallas kernels, merge_keys(): pl.pallas_call(merge_keys_kernel, in_specs=[SMEM, hbm, hbm], out_specs=[h...  4.13 us
  transfers between devices with their start and end apart: 8, of which 4 were waited for; matrix products, arithmetic and copies ran while one was open for 1% of the time, Pallas kernels for 3%

profile of v1, /device:TPU:1, one launch (start us, length us, event | category | flops | bytes accessed | tf_op | source)
XLA Modules:
  0.0 187.5 jit_solution(13866129342510155642)
XLA Ops:
  0.6 0.0 copy-start
  0.6 0.0 copy-start.1
  0.7 3.1 %shard_map.102 = (s32[16]{0:T(128)S(1)}, bf16[2,576,256]{2,1,0:T(8,128)(2,1)S(1)}, bf16[2,576,256]{2,1,0:T(8,128)(2,1)S(1)}) custom-call(s32[1]{0:T(128)} %bitcast.own_ref, s32[2,64]{1,0:T(2,128)} %bitcast.6, s32[2,64]{1,0:T(2,128)} %bitcast.7, s32[2,64]{1,0:T(2,128)} %bitcast.8, bf16[1152,256]{1,0:T(8,128)(2,1)} %k_hbm.1, bf16[1152,256]{1,0:T(8,128)(2,1)} %v_hbm.1), custom_call_target="tpu_custom_call" | custom-call | tf_op jit(solution)/shard_map/pallas_call | solution.py:91
  3.7 0.6 fusion
  5.6 0.0 copy-done
  5.6 0.0 copy-done.1
  5.6 86.7 %conditional.29 = (bf16[2,576,256]{2,1,0:T(8,128)(2,1)}, bf16[2,576,256]{2,1,0:T(8,128)(2,1)}, bf16[2,512,256]{2,1,0:T(8,128)(2,1)}, bf16[2,512,256]{2,1,0:T(8,128)(2,1)}) conditional(s32[]{:T(128)} %bitcast.4, (bf16[2,576,256]{2,1,0:T(8,128)(2,1)S(1)}, bf16[2,576,256]{2,1,0:T(8,128)(2,1)S(1)}, s32[]{:T(128)}, ...), branch_computations={%region_0.0_spmd, %region_3.0_spmd, %region_13.0_spmd, %region_16.... | conditional | flops 3 | bytes 15204622 | solution.py:335
  5.7 14.6 %collective-permute-start.13 = (bf16[2,576,256]{2,1,0:T(8,128)(2,1)S(1)}, bf16[2,576,256]{2,1,0:T(8,128)(2,1)}, u32[]{:S(2)}, u32[]{:S(2)}) collective-permute-start(bf16[2,576,256]{2,1,0:T(8,128)(2,1)S(1)} %get-tuple-element.534), channel_id=1, source_target_pairs={{0,496},{8,504},{16,0},{24,8},{32,16},{40,24},{48,32},{56,40},{64,... | collective-permute-start | bytes 1769480 | tf_op jit(solution)/shard_map/cond/branch_1_fun/ppermute | solution.py:31
  20.3 1.9 %collective-permute-start.14 = (bf16[2,576,256]{2,1,0:T(8,128)(2,1)S(1)}, bf16[2,576,256]{2,1,0:T(8,128)(2,1)}, u32[]{:S(2)}, u32[]{:S(2)}) collective-permute-start(bf16[2,576,256]{2,1,0:T(8,128)(2,1)S(1)} %get-tuple-element.535), channel_id=1, source_target_pairs={{0,16},{8,24},{16,32},{24,40},{32,48},{40,56},{48,64},{56,72},{64,... | collective-permute-start | bytes 1769480 | tf_op jit(solution)/shard_map/cond/branch_1_fun/ppermute | solution.py:31
  23.5 0.1 branch_1_fun.4
  23.6 20.8 %conditional.1 = (bf16[8,2,128,256]{3,2,1,0:T(8,128)(2,1)S(1)}) conditional(s32[]{:T(128)} %convert_element_type.45, bf16[8,2,128,256]{3,2,1,0:T(8,128)(2,1)S(1)} %branch_1_fun.4, bf16[8,2,128,256]{3,2,1,0:T(8,128)(2,1)S(1)} %branch_1_fun.4), branch_computations={%region_4.0_spmd, %region_5.0_spmd} | conditional | bytes 4194312 | solution.py:287
  23.6 0.1 copy.214
  23.7 20.7 %all_to_all.89 = bf16[8,2,128,256]{3,2,1,0:T(8,128)(2,1)S(1)} all-to-all(bf16[8,2,128,256]{3,2,1,0:T(8,128)(2,1)S(1)} %copy.214), channel_id=1, replica_groups=mesh['dp'=64,'mp'=8] {'mp'}, dimensions={0} | all-to-all | bytes 2097152 | tf_op jit(solution)/shard_map/cond/branch_1_fun/cond/branch_1_fun/all_to_all | solution.py:285
  44.4 2.8 %branch_1_fun.5 = (bf16[2,512,256]{2,1,0:T(8,128)(2,1)}, bf16[2,512,256]{2,1,0:T(8,128)(2,1)}) custom-call(s32[16]{0:T(128)S(1)} %get-tuple-element.537.scal, bf16[8,2,128,256]{3,2,1,0:T(8,128)(2,1)S(1)} %get-tuple-element.961.in_ref), custom_call_target="tpu_custom_call" | custom-call | tf_op jit(solution)/shard_map/cond/branch_1_fun/pallas_call | solution.py:153
  47.1 45.1 %conditional.2 = ((bf16[2,512,256]{2,1,0:T(8,128)(2,1)}, bf16[2,512,256]{2,1,0:T(8,128)(2,1)})) conditional(s32[]{:T(128)} %clamp.15, (bf16[2,512,256]{2,1,0:T(8,128)(2,1)}, bf16[2,512,256]{2,1,0:T(8,128)(2,1)}) %tuple.259, (bf16[2,512,256]{2,1,0:T(8,128)(2,1)}, bf16[2,512,256]{2,1,0:T(8,128)(2,1)}) %tuple.259, ...), branch_computations={%region_6.0_spmd, %region_7.0_spmd, %region_8.0_spmd, %region_9.0_... | conditional | bytes 6291560 | solution.py:330
  47.1 1.9 %collective-permute-start.7 = (bf16[2,512,256]{2,1,0:T(8,128)(2,1)}, bf16[2,512,256]{2,1,0:T(8,128)(2,1)S(1)}, u32[]{:S(2)}, u32[]{:S(2)}) collective-permute-start(bf16[2,512,256]{2,1,0:T(8,128)(2,1)} %get-tuple-element.528), channel_id=1, source_target_pairs={{0,32},{8,40},{16,48},{24,56},{32,64},{40,72},{48,80},{56,88},{64,... | collective-permute-start | bytes 1572872 | tf_op jit(solution)/shard_map/cond/branch_1_fun/cond/branch_4_fun/ppermute | solution.py:31
  49.0 8.9 %collective-permute-start.8 = (bf16[2,512,256]{2,1,0:T(8,128)(2,1)}, bf16[2,512,256]{2,1,0:T(8,128)(2,1)S(1)}, u32[]{:S(2)}, u32[]{:S(2)}) collective-permute-start(bf16[2,512,256]{2,1,0:T(8,128)(2,1)} %get-tuple-element.529), channel_id=1, source_target_pairs={{0,488},{8,496},{16,504},{24,0},{32,8},{40,16},{48,24},{56,32},{64... | collective-permute-start | bytes 1572872 | tf_op jit(solution)/shard_map/cond/branch_1_fun/cond/branch_4_fun/ppermute | solution.py:31
  58.0 15.0 %collective-permute-done.7 = bf16[2,512,256]{2,1,0:T(8,128)(2,1)S(1)} collective-permute-done((bf16[2,512,256]{2,1,0:T(8,128)(2,1)}, bf16[2,512,256]{2,1,0:T(8,128)(2,1)S(1)}, u32[]{:S(2)}, u32[]{:S(2)}) %collective-permute-start.7) | collective-permute-done | bytes 524320 | tf_op jit(solution)/shard_map/cond/branch_1_fun/cond/branch_4_fun/ppermute | solution.py:31
  73.0 0.8 copy.23
  73.8 17.7 %collective-permute-done.8 = bf16[2,512,256]{2,1,0:T(8,128)(2,1)S(1)} collective-permute-done((bf16[2,512,256]{2,1,0:T(8,128)(2,1)}, bf16[2,512,256]{2,1,0:T(8,128)(2,1)S(1)}, u32[]{:S(2)}, u32[]{:S(2)}) %collective-permute-start.8) | collective-permute-done | bytes 524320 | tf_op jit(solution)/shard_map/cond/branch_1_fun/cond/branch_4_fun/ppermute | solution.py:31
  91.5 0.8 copy.24
  92.3 0.0 collective-permute-done.13
  92.3 0.0 collective-permute-done.14
  92.3 5.1 %shard_map.103 = (bf16[2,512,256]{2,1,0:T(8,128)(2,1)S(1)}, bf16[2,512,256]{2,1,0:T(8,128)(2,1)S(1)}, bf16[2,576,256]{2,1,0:T(8,128)(2,1)S(1)}, bf16[2,576,256]{2,1,0:T(8,128)(2,1)S(1)}) custom-call(s32[16]{0:T(128)S(1)} %get-tuple-element.781.scal, bf16[2,512,256]{2,1,0:T(8,128)(2,1)} %get-tuple-element.784.xm_ref, ...), custom_call_target="tpu_custom_call" | custom-call | flops 1811939328 | bytes 5242880 | tf_op jit(solution)/shard_map/pallas_call | solution.py:272
  97.4 52.5 %conditional.30 = ((bf16[2,512,256]{2,1,0:T(8,128)(2,1)S(1)}, bf16[2,512,256]{2,1,0:T(8,128)(2,1)S(1)})) conditional(s32[]{:T(128)} %clamp.24, (bf16[2,512,256]{2,1,0:T(8,128)(2,1)S(1)}, bf16[2,512,256]{2,1,0:T(8,128)(2,1)S(1)}) %tuple.364, (bf16[2,512,256]{2,1,0:T(8,128)(2,1)S(1)}, ...), branch_computations={%region_61.0_spmd, %region_62.0_spmd, %region_63.0_spmd, %region_6... | conditional | bytes 6291560 | solution.py:349
  97.4 5.2 %collective-permute-start.71 = (bf16[2,512,256]{2,1,0:T(8,128)(2,1)S(1)}, bf16[2,512,256]{2,1,0:T(8,128)(2,1)S(1)}, u32[]{:S(2)}, u32[]{:S(2)}) collective-permute-start(bf16[2,512,256]{2,1,0:T(8,128)(2,1)S(1)} %get-tuple-element.664), channel_id=1, source_target_pairs={{0,480},{8,488},{16,496},{24,504},{32,0},{40,8},{48,16},{56,24},{6... | collective-permute-start | bytes 1572872 | tf_op jit(solution)/shard_map/cond/branch_4_fun/ppermute | solution.py:31
  102.6 14.7 %collective-permute-start.72 = (bf16[2,512,256]{2,1,0:T(8,128)(2,1)S(1)}, bf16[2,512,256]{2,1,0:T(8,128)(2,1)S(1)}, u32[]{:S(2)}, u32[]{:S(2)}) collective-permute-start(bf16[2,512,256]{2,1,0:T(8,128)(2,1)S(1)} %get-tuple-element.665), channel_id=1, source_target_pairs={{0,24},{8,32},{16,40},{24,48},{32,56},{40,64},{48,72},{56,80},{64,... | collective-permute-start | bytes 1572872 | tf_op jit(solution)/shard_map/cond/branch_4_fun/ppermute | solution.py:31
  117.3 32.5 %collective-permute-done.71 = bf16[2,512,256]{2,1,0:T(8,128)(2,1)S(1)} collective-permute-done((bf16[2,512,256]{2,1,0:T(8,128)(2,1)S(1)}, bf16[2,512,256]{2,1,0:T(8,128)(2,1)S(1)}, u32[]{:S(2)}, u32[]{:S(2)}) %collective-permute-start.71) | collective-permute-done | bytes 524320 | tf_op jit(solution)/shard_map/cond/branch_4_fun/ppermute | solution.py:31
  149.9 0.0 collective-permute-done.72
  150.0 33.2 %conditional.31 = (bf16[2,576,256]{2,1,0:T(8,128)(2,1)}, bf16[2,576,256]{2,1,0:T(8,128)(2,1)}, bf16[128,2048]{1,0:T(8,128)(2,1)}, bf16[128,2048]{1,0:T(8,128)(2,1)}) conditional(s32[]{:T(128)} %bitcast.4, (bf16[2,576,256]{2,1,0:T(8,128)(2,1)S(1)}, bf16[2,576,256]{2,1,0:T(8,128)(2,1)S(1)}, s32[]{:T(128)}, ...), branch_computations={%region_68.0_spmd, %region_71.0_spmd, %region_74.0_spmd, %region_7... | conditional | flops 2 | bytes 8913030 | solution.py:360
  150.0 1.9 %collective-permute-start.79 = (bf16[2,576,256]{2,1,0:T(8,128)(2,1)S(1)}, bf16[2,576,256]{2,1,0:T(8,128)(2,1)}, u32[]{:S(2)}, u32[]{:S(2)}) collective-permute-start(bf16[2,576,256]{2,1,0:T(8,128)(2,1)S(1)} %get-tuple-element.678), channel_id=1, source_target_pairs={{0,16},{8,24},{16,32},{24,40},{32,48},{40,56},{48,64},{56,72},{64,... | collective-permute-start | bytes 1769480 | tf_op jit(solution)/shard_map/cond/branch_1_fun/ppermute | solution.py:31
  151.9 7.6 %collective-permute-start.80 = (bf16[2,576,256]{2,1,0:T(8,128)(2,1)S(1)}, bf16[2,576,256]{2,1,0:T(8,128)(2,1)}, u32[]{:S(2)}, u32[]{:S(2)}) collective-permute-start(bf16[2,576,256]{2,1,0:T(8,128)(2,1)S(1)} %get-tuple-element.679), channel_id=1, source_target_pairs={{0,496},{8,504},{16,0},{24,8},{32,16},{40,24},{48,32},{56,40},{64,... | collective-permute-start | bytes 1769480 | tf_op jit(solution)/shard_map/cond/branch_1_fun/ppermute | solution.py:31
  160.2 2.5 %branch_1_fun.6 = bf16[8,2,128,256]{3,2,1,0:T(8,128)(2,1)S(1)} custom-call(s32[16]{0:T(128)S(1)} %get-tuple-element.681.scal, bf16[2,512,256]{2,1,0:T(8,128)(2,1)S(1)} %get-tuple-element.682.a_ref, bf16[2,512,256]{2,1,0:T(8,128)(2,1)S(1)} %get-tuple-element.683.b_ref), custom_call_target="tpu_custom_call" | custom-call | tf_op jit(solution)/shard_map/cond/branch_1_fun/pallas_call | solution.py:183
  162.7 19.1 %conditional.16 = (bf16[8,2,128,256]{3,2,1,0:T(8,128)(2,1)S(1)}) conditional(s32[]{:T(128)} %convert_element_type.56, bf16[8,2,128,256]{3,2,1,0:T(8,128)(2,1)S(1)} %branch_1_fun.6, bf16[8,2,128,256]{3,2,1,0:T(8,128)(2,1)S(1)} %branch_1_fun.6), branch_computations={%region_72.0_spmd, %region_73.0_spmd} | conditional | bytes 4194312 | solution.py:287
  162.7 0.1 copy.225
  162.8 19.0 %all_to_all.100 = bf16[8,2,128,256]{3,2,1,0:T(8,128)(2,1)S(1)} all-to-all(bf16[8,2,128,256]{3,2,1,0:T(8,128)(2,1)S(1)} %copy.225), channel_id=1, replica_groups=mesh['dp'=64,'mp'=8] {'mp'}, dimensions={0} | all-to-all | bytes 2097152 | tf_op jit(solution)/shard_map/cond/branch_1_fun/cond/branch_1_fun/all_to_all | solution.py:285
  181.8 1.1 branch_1_fun.7
  182.9 0.2 collective-permute-done.79
  183.2 0.0 collective-permute-done.80
  183.2 4.1 %shard_map.104 = (bf16[1152,256]{1,0:T(8,128)(2,1)}, bf16[1152,256]{1,0:T(8,128)(2,1)}) custom-call(s32[16]{0:T(128)S(1)} %get-tuple-element.781.scal, bf16[2,576,256]{2,1,0:T(8,128)(2,1)} %get-tuple-element.796.a_hbm, bf16[2,576,256]{2,1,0:T(8,128)(2,1)} %get-tuple-element.797.b_hbm), custom_call_target="tpu_custom_call" | custom-call | tf_op jit(solution)/shard_map/pallas_call | solution.py:223
  (2 shorter events, 0.1 us)
Async XLA Ops:
  0.6 5.0 %copy-start = (bf16[128,2048]{1,0:T(8,128)(2,1)S(1)}, bf16[128,2048]{1,0:T(8,128)(2,1)}, u32[]{:S(2)}) copy-start(bf16[128,2048]{1,0:T(8,128)(2,1)} %param.108) | copy-start | bytes 1572868
  0.6 5.0 %copy-start.1 = (bf16[128,2048]{1,0:T(8,128)(2,1)S(1)}, bf16[128,2048]{1,0:T(8,128)(2,1)}, u32[]{:S(2)}) copy-start(bf16[128,2048]{1,0:T(8,128)(2,1)} %param.111) | copy-start | bytes 1572868
  5.7 86.6 %collective-permute-start.13 = (bf16[2,576,256]{2,1,0:T(8,128)(2,1)S(1)}, bf16[2,576,256]{2,1,0:T(8,128)(2,1)}, u32[]{:S(2)}, u32[]{:S(2)}) collective-permute-start(bf16[2,576,256]{2,1,0:T(8,128)(2,1)S(1)} %get-tuple-element.534), channel_id=1, source_target_pairs={{0,496},{8,504},{16,0},{24,8},{32,16},{40,24},{48,32},{56,40},{64,... | collective-permute-start | bytes 1769480 | tf_op jit(solution)/shard_map/cond/branch_1_fun/ppermute | solution.py:31
  20.3 72.0 %collective-permute-start.14 = (bf16[2,576,256]{2,1,0:T(8,128)(2,1)S(1)}, bf16[2,576,256]{2,1,0:T(8,128)(2,1)}, u32[]{:S(2)}, u32[]{:S(2)}) collective-permute-start(bf16[2,576,256]{2,1,0:T(8,128)(2,1)S(1)} %get-tuple-element.535), channel_id=1, source_target_pairs={{0,16},{8,24},{16,32},{24,40},{32,48},{40,56},{48,64},{56,72},{64,... | collective-permute-start | bytes 1769480 | tf_op jit(solution)/shard_map/cond/branch_1_fun/ppermute | solution.py:31
  47.1 25.9 %collective-permute-start.7 = (bf16[2,512,256]{2,1,0:T(8,128)(2,1)}, bf16[2,512,256]{2,1,0:T(8,128)(2,1)S(1)}, u32[]{:S(2)}, u32[]{:S(2)}) collective-permute-start(bf16[2,512,256]{2,1,0:T(8,128)(2,1)} %get-tuple-element.528), channel_id=1, source_target_pairs={{0,32},{8,40},{16,48},{24,56},{32,64},{40,72},{48,80},{56,88},{64,... | collective-permute-start | bytes 1572872 | tf_op jit(solution)/shard_map/cond/branch_1_fun/cond/branch_4_fun/ppermute | solution.py:31
  49.0 42.4 %collective-permute-start.8 = (bf16[2,512,256]{2,1,0:T(8,128)(2,1)}, bf16[2,512,256]{2,1,0:T(8,128)(2,1)S(1)}, u32[]{:S(2)}, u32[]{:S(2)}) collective-permute-start(bf16[2,512,256]{2,1,0:T(8,128)(2,1)} %get-tuple-element.529), channel_id=1, source_target_pairs={{0,488},{8,496},{16,504},{24,0},{32,8},{40,16},{48,24},{56,32},{64... | collective-permute-start | bytes 1572872 | tf_op jit(solution)/shard_map/cond/branch_1_fun/cond/branch_4_fun/ppermute | solution.py:31
  97.4 52.4 %collective-permute-start.71 = (bf16[2,512,256]{2,1,0:T(8,128)(2,1)S(1)}, bf16[2,512,256]{2,1,0:T(8,128)(2,1)S(1)}, u32[]{:S(2)}, u32[]{:S(2)}) collective-permute-start(bf16[2,512,256]{2,1,0:T(8,128)(2,1)S(1)} %get-tuple-element.664), channel_id=1, source_target_pairs={{0,480},{8,488},{16,496},{24,504},{32,0},{40,8},{48,16},{56,24},{6... | collective-permute-start | bytes 1572872 | tf_op jit(solution)/shard_map/cond/branch_4_fun/ppermute | solution.py:31
  102.6 47.3 %collective-permute-start.72 = (bf16[2,512,256]{2,1,0:T(8,128)(2,1)S(1)}, bf16[2,512,256]{2,1,0:T(8,128)(2,1)S(1)}, u32[]{:S(2)}, u32[]{:S(2)}) collective-permute-start(bf16[2,512,256]{2,1,0:T(8,128)(2,1)S(1)} %get-tuple-element.665), channel_id=1, source_target_pairs={{0,24},{8,32},{16,40},{24,48},{32,56},{40,64},{48,72},{56,80},{64,... | collective-permute-start | bytes 1572872 | tf_op jit(solution)/shard_map/cond/branch_4_fun/ppermute | solution.py:31
  150.0 33.2 %collective-permute-start.79 = (bf16[2,576,256]{2,1,0:T(8,128)(2,1)S(1)}, bf16[2,576,256]{2,1,0:T(8,128)(2,1)}, u32[]{:S(2)}, u32[]{:S(2)}) collective-permute-start(bf16[2,576,256]{2,1,0:T(8,128)(2,1)S(1)} %get-tuple-element.678), channel_id=1, source_target_pairs={{0,16},{8,24},{16,32},{24,40},{32,48},{40,56},{48,64},{56,72},{64,... | collective-permute-start | bytes 1769480 | tf_op jit(solution)/shard_map/cond/branch_1_fun/ppermute | solution.py:31
  151.9 31.3 %collective-permute-start.80 = (bf16[2,576,256]{2,1,0:T(8,128)(2,1)S(1)}, bf16[2,576,256]{2,1,0:T(8,128)(2,1)}, u32[]{:S(2)}, u32[]{:S(2)}) collective-permute-start(bf16[2,576,256]{2,1,0:T(8,128)(2,1)S(1)} %get-tuple-element.679), channel_id=1, source_target_pairs={{0,496},{8,504},{16,0},{24,8},{32,16},{40,24},{48,32},{56,40},{64,... | collective-permute-start | bytes 1769480 | tf_op jit(solution)/shard_map/cond/branch_1_fun/ppermute | solution.py:31
